TPU v7x, 256 devices: a whole 4x4x8 slice. The times are simulated.
256 devices in a mesh: seq: 16 (over z, core), head: 4 (over x), dp: 4 (over y).
Axes of the slice: x: 4, y: 4, z: 8, core: 2. Of those that a mesh axis runs over, the one named last changes fastest.
Arguments:
- self_queries: bfloat16 [4, 2048, 2560], P('dp', ('seq', 'head')), may hold values from -8 to 8
- self_keys: bfloat16 [4, 2048, 2560], P('dp', ('seq', 'head')), may hold values from -4 to 4
- self_values: bfloat16 [4, 2048, 2560], P('dp', ('seq', 'head')), may hold values from -6 to 6
- self_cotangent: bfloat16 [4, 2048, 2560], P('dp', ('seq', 'head')), may hold values from -6 to 6
- text_queries: bfloat16 [4, 4096, 2560], P('dp', 'seq', 'head'), may hold values from -8 to 8
- memory_keys: bfloat16 [4, 2048, 2560], P('dp', 'seq', 'head'), may hold values from -4 to 4
- memory_values: bfloat16 [4, 2048, 2560], P('dp', 'seq', 'head'), may hold values from -6 to 6
- text_cotangent: bfloat16 [4, 4096, 2560], P('dp', 'seq', 'head'), may hold values from -6 to 6
- slopes: float32 [2, 20], P(None, 'head'), may hold values from 0.01 to 0.3
- page_counts: int32 [4, 4], P('dp'), may hold values from 1 to 1024, as said below
- page_cols: int32 [4, 4], P('dp'), may hold values from 4 to 64
- text_page: int32 [4, 4096], P('dp'), may hold values from 0 to 3, as said below
Outputs:
- self_query_grad: bfloat16 [4, 2048, 2560], P('dp', ('seq', 'head'))
- self_key_grad: bfloat16 [4, 2048, 2560], P('dp', ('seq', 'head'))
- self_value_grad: bfloat16 [4, 2048, 2560], P('dp', ('seq', 'head'))
- slope_grad: float32 [2, 20], P(None, 'head')
- text_query_grad: bfloat16 [4, 4096, 2560], P('dp', 'seq', 'head')
- memory_key_grad: bfloat16 [4, 2048, 2560], P('dp', 'seq', 'head')
- memory_value_grad: bfloat16 [4, 2048, 2560], P('dp', 'seq', 'head')
Inputs may be any that keep to these rules, and one draw needn't show every extreme that they name: `page_counts`: each pack's counts sum to 2048; one page of every pack has exactly 1024 patches. `text_page`: never falls along a pack's text rows; every page has at least one text row.
All inputs are finite; a program needn't handle non-finite values.
Results may differ from a plain program's by a relative error of at most 0.006.
Values may be sent and summed in bfloat16 or wider, within the bound.
No kernel may reach another device: no remote copies, remote signals or barrier semaphores. Data moves between devices by JAX's collectives and lax.ppermute only.
A program may use at most 128 MiB of HBM per device.

v0:
```python
import jax
import jax.numpy as jnp
from jax import lax
from jax.sharding import PartitionSpec as P

MASK_FILL = -1e30


def page_layout(counts, widths, patch_total):
    page_ends = jnp.cumsum(counts)
    starts = page_ends - counts
    positions = jnp.arange(patch_total, dtype=jnp.int32)
    page_ids = jnp.sum((positions[:, None] >= page_ends[None, :]).astype(jnp.int32), axis=1)
    one_hot = page_ids[:, None] == jnp.arange(counts.shape[0], dtype=jnp.int32)[None, :]
    page_start = jnp.sum(jnp.where(one_hot, starts[None, :], 0), axis=1)
    page_width = jnp.sum(jnp.where(one_hot, widths[None, :], 0), axis=1)
    offsets = positions - page_start
    return (page_ids, offsets // page_width, offsets % page_width)


def take_rows(vector, row_start, row_count):
    return lax.dynamic_slice_in_dim(vector, row_start, row_count, 0)


def heads_of(matrix, head_count):
    return matrix.reshape(matrix.shape[0], head_count, -1)


def alibi(slopes, query_layout, key_layout):
    row_gap = jnp.abs(query_layout[1][:, None] - key_layout[1][None, :]).astype(jnp.float32)
    col_gap = jnp.abs(query_layout[2][:, None] - key_layout[2][None, :]).astype(jnp.float32)
    same_page = query_layout[0][:, None] == key_layout[0][None, :]
    decay = -(slopes[0][:, None, None] * row_gap[None] + slopes[1][:, None, None] * col_gap[None])
    return (jnp.where(same_page[None], decay, MASK_FILL), row_gap, col_gap)


def query_side(queries, key_rows, value_rows, grad_rows, logit_bias):
    inv_root = queries.shape[2] ** (-0.5)
    scores = (
        jnp.einsum("rhs,khs->hrk", queries, key_rows, preferred_element_type=jnp.float32) * inv_root
        + logit_bias
    )
    row_max = jnp.max(scores, axis=2, keepdims=True)
    weights = jnp.exp(scores - row_max)
    row_total = jnp.sum(weights, axis=2, keepdims=True)
    softmax_w = weights / row_total
    log_total = (row_max + jnp.log(row_total))[:, :, 0]
    grad_probs = jnp.einsum(
        "rhs,khs->hrk", grad_rows, value_rows, preferred_element_type=jnp.float32
    )
    row_delta = jnp.sum(softmax_w * grad_probs, axis=2, keepdims=True)
    grad_scores = softmax_w * (grad_probs - row_delta)
    grad_scores_b = grad_scores.astype(jnp.bfloat16)
    query_grad = (
        jnp.einsum("hrk,khs->rhs", grad_scores_b, key_rows, preferred_element_type=jnp.float32)
        * inv_root
    )
    return (
        query_grad,
        grad_scores,
        grad_scores_b,
        softmax_w.astype(jnp.bfloat16),
        log_total,
        row_delta[:, :, 0],
    )


def key_terms(grad_scores_b, softmax_b, queries, grad_rows, row_count):
    inv_root = queries.shape[3] ** (-0.5)
    key_grad = (
        jnp.einsum("chrk,crhs->khs", grad_scores_b, queries, preferred_element_type=jnp.float32)
        * inv_root
    )
    value_grad = jnp.einsum(
        "chrk,crhs->khs", softmax_b, grad_rows, preferred_element_type=jnp.float32
    )
    return jnp.stack([key_grad.reshape(row_count, -1), value_grad.reshape(row_count, -1)], axis=1)


def local(
    self_queries,
    self_keys,
    self_values,
    self_cotangent,
    text_queries,
    memory_keys,
    memory_values,
    text_cotangent,
    slopes,
    page_counts,
    page_cols,
    text_page,
):
    head_count = slopes.shape[1]
    regrouped = (
        lax.all_to_all(self_queries[0], "head", split_axis=1, concat_axis=0, tiled=True),
        lax.all_to_all(self_keys[0], "head", split_axis=1, concat_axis=0, tiled=True),
        lax.all_to_all(self_values[0], "head", split_axis=1, concat_axis=0, tiled=True),
        lax.all_to_all(self_cotangent[0], "head", split_axis=1, concat_axis=0, tiled=True),
    )
    local_queries, local_keys, local_values, local_grads = regrouped
    patch_rows = local_queries.shape[0]
    all_keys, all_values = (
        lax.all_gather(local_keys, "seq", axis=0, tiled=True),
        lax.all_gather(local_values, "seq", axis=0, tiled=True),
    )
    patch_total = all_keys.shape[0]
    whole_layout = page_layout(page_counts[0], page_cols[0], patch_total)
    own_start = lax.axis_index("seq") * patch_rows
    own_layout = tuple((take_rows(item, own_start, patch_rows) for item in whole_layout))
    self_bias, row_gap, col_gap = alibi(slopes, own_layout, whole_layout)
    query_heads = heads_of(local_queries, head_count)
    grad_heads = heads_of(local_grads, head_count)
    self_dq, self_ds, self_ds_b, self_p_b, self_lse, self_delta = query_side(
        query_heads,
        heads_of(all_keys, head_count),
        heads_of(all_values, head_count),
        grad_heads,
        self_bias,
    )
    slope_local = -jnp.stack(
        [
            jnp.sum(self_ds * row_gap[None], axis=(1, 2)),
            jnp.sum(self_ds * col_gap[None], axis=(1, 2)),
        ]
    )
    self_ds_blocks = self_ds_b[None]
    self_p_blocks = self_p_b[None]
    query_blocks = query_heads[None]
    grad_blocks = grad_heads[None]
    self_pair = lax.psum_scatter(
        key_terms(
            self_ds_blocks,
            self_p_blocks,
            query_blocks,
            grad_blocks,
            patch_rows * lax.axis_size("seq"),
        ),
        "seq",
        scatter_dimension=0,
        tiled=True,
    )
    self_dk = self_pair[:, 0]
    self_dv = self_pair[:, 1]
    restored = (
        lax.all_to_all(
            self_dq.reshape(patch_rows, -1).astype(jnp.bfloat16),
            "head",
            split_axis=0,
            concat_axis=1,
            tiled=True,
        ),
        lax.all_to_all(
            self_dk.astype(jnp.bfloat16), "head", split_axis=0, concat_axis=1, tiled=True
        ),
        lax.all_to_all(
            self_dv.astype(jnp.bfloat16), "head", split_axis=0, concat_axis=1, tiled=True
        ),
    )
    slope_grad = lax.psum(slope_local, ("seq", "dp")) / patch_total
    memory_all_keys, memory_all_values = (
        lax.all_gather(memory_keys[0], "seq", axis=0, tiled=True),
        lax.all_gather(memory_values[0], "seq", axis=0, tiled=True),
    )
    memory_all_key_heads = heads_of(memory_all_keys, head_count)
    memory_all_value_heads = heads_of(memory_all_values, head_count)
    text_rows = text_queries.shape[1]
    text_start = lax.axis_index("seq") * text_rows
    text_ids = text_page[0]
    own_text = take_rows(text_ids, text_start, text_rows)
    text_query_heads = heads_of(text_queries[0], head_count)
    text_grad_heads = heads_of(text_cotangent[0], head_count)
    block_count = text_rows // text_rows
    text_query_blocks = text_query_heads.reshape(block_count, text_rows, head_count, -1)
    text_grad_blocks = text_grad_heads.reshape(block_count, text_rows, head_count, -1)

    def cross_block(inputs):
        block_queries, block_grads, block_pages = inputs
        block_bias = jnp.where(
            block_pages[:, None] == whole_layout[0][None, :], 0.0, MASK_FILL
        ).astype(jnp.float32)[None]
        result = query_side(
            block_queries, memory_all_key_heads, memory_all_value_heads, block_grads, block_bias
        )
        return (result[0], result[2], result[3], result[4], result[5])

    cross_out = lax.map(
        cross_block, (text_query_blocks, text_grad_blocks, own_text.reshape(block_count, text_rows))
    )
    text_dq = cross_out[0].reshape(text_rows, -1)
    text_ds_b = cross_out[1]
    text_p_b = cross_out[2]
    memory_pair = lax.psum_scatter(
        key_terms(
            text_ds_b,
            text_p_b,
            text_query_blocks,
            text_grad_blocks,
            patch_rows * lax.axis_size("seq"),
        ),
        "seq",
        scatter_dimension=0,
        tiled=True,
    )
    memory_dk = memory_pair[:, 0]
    memory_dv = memory_pair[:, 1]
    return (
        restored[0][None],
        restored[1][None],
        restored[2][None],
        slope_grad,
        text_dq.astype(jnp.bfloat16)[None],
        memory_dk.astype(jnp.bfloat16)[None],
        memory_dv.astype(jnp.bfloat16)[None],
    )


def solution(mesh):
    in_specs = (
        P("dp", ("seq", "head"), None),
        P("dp", ("seq", "head"), None),
        P("dp", ("seq", "head"), None),
        P("dp", ("seq", "head"), None),
        P("dp", "seq", "head"),
        P("dp", "seq", "head"),
        P("dp", "seq", "head"),
        P("dp", "seq", "head"),
        P(None, "head"),
        P("dp", None),
        P("dp", None),
        P("dp", None),
    )
    out_specs = (
        P("dp", ("seq", "head"), None),
        P("dp", ("seq", "head"), None),
        P("dp", ("seq", "head"), None),
        P(None, "head"),
        P("dp", "seq", "head"),
        P("dp", "seq", "head"),
        P("dp", "seq", "head"),
    )
    return jax.shard_map(local, mesh=mesh, in_specs=in_specs, out_specs=out_specs, check_vma=False)
```

profile of v0, /device:TPU:2, one launch (start us, length us, event | category | flops | bytes accessed | tf_op | source)
XLA Modules:
  0.0 406.0 jit_solution(9305916653580052399)
XLA Ops:
  8.3 10.0 %all_to_all.109 = bf16[32,4,640]{2,0,1:T(8,128)(2,1)} all-to-all(bf16[32,4,640]{2,0,1:T(8,128)(2,1)S(1)} %copy.117), channel_id=1, replica_groups=mesh['seq'=16,'head'=4,'dp'=4] {'head'}, dimensions={1} | all-to-all | bytes 327680 | tf_op jit(solution)/shard_map/all_to_all | solution.py:97
  19.4 9.2 %all_to_all.110 = bf16[32,4,640]{2,0,1:T(8,128)(2,1)} all-to-all(bf16[32,4,640]{2,0,1:T(8,128)(2,1)S(1)} %copy.122), channel_id=1, replica_groups=mesh['seq'=16,'head'=4,'dp'=4] {'head'}, dimensions={1} | all-to-all | bytes 327680 | tf_op jit(solution)/shard_map/all_to_all | solution.py:98
  32.1 4.7 %all-to-all-start = ((bf16[32,4,640]{2,0,1:T(8,128)(2,1)}), bf16[32,4,640]{2,0,1:T(8,128)(2,1)S(1)}, u32[]{:S(2)}, u32[]{:S(2)}) async-start(bf16[32,4,640]{2,0,1:T(8,128)(2,1)} %copy.116), calls=%async_computation | async-start | bytes 327680 | tf_op jit(solution)/shard_map/all_to_all | solution.py:96
  44.2 4.8 %all-to-all-start.2 = ((bf16[32,4,640]{2,0,1:T(8,128)(2,1)}), bf16[32,4,640]{2,0,1:T(8,128)(2,1)S(1)}, u32[]{:S(2)}, u32[]{:S(2)}) async-start(bf16[32,4,640]{2,0,1:T(8,128)(2,1)} %copy.121), calls=%async_computation.2 | async-start | bytes 327680 | tf_op jit(solution)/shard_map/all_to_all | solution.py:99
  49.4 4.3 %all-to-all-done.2 = bf16[32,4,640]{2,0,1:T(8,128)(2,1)S(1)} async-done(((bf16[32,4,640]{2,0,1:T(8,128)(2,1)}), bf16[32,4,640]{2,0,1:T(8,128)(2,1)S(1)}, u32[]{:S(2)}, u32[]{:S(2)}) %all-to-all-start.2) | async-done | bytes 163872 | tf_op jit(solution)/shard_map/all_to_all | solution.py:99
  54.1 6.2 %all-gather.7.cloned.1.call-done = bf16[2048,640]{1,0:T(8,128)(2,1)} async-done(((bf16[128,640]{1,0:T(8,128)(2,1)}), bf16[2048,640]{1,0:T(8,128)(2,1)}) %all-gather.7.cloned.1.call-update) | async-done | bytes 2621456 | tf_op jit(solution)/shard_map/all_gather | solution.py:104
  63.3 37.8 %all-gather.9.cloned.1.call-done = bf16[2048,640]{1,0:T(8,128)(2,1)} async-done(((bf16[128,640]{1,0:T(8,128)(2,1)}), bf16[2048,640]{1,0:T(8,128)(2,1)}) %all-gather.9.cloned.1.call-update) | async-done | bytes 2621456 | tf_op jit(solution)/shard_map/all_gather | solution.py:105
  101.0 4.5 %copy.123 = bf16[2048,640]{0,1:T(8,128)(2,1)} copy(bf16[2048,640]{1,0:T(8,128)(2,1)} %all-gather.9.cloned.1.call-done) | data formatting | bytes 5242880 | tf_op jit(solution)/shard_map/all_gather | solution.py:105
  119.8 6.0 %copy.131 = f32[2048,1,640]{2,0,1:T(8,128)} copy(f32[2048,1,640]{0,2,1:T(8,128)} %bitcast.79) | data formatting | bytes 10485760 | tf_op jit(solution)/shard_map/stack;reshape | solution.py:77
  125.8 8.0 %fusion.7 = f32[5,2048,128]{1,2,0:T(8,128)} fusion(bf16[128,5,128]{0,2,1:T(8,128)(2,1)S(1)} %copy.130, f32[5,128]{1,0:T(8,128)S(1)} %get-tuple-element.85, f32[5,128,2048]{2,1,0:T(8,128)} %copy-done.4), kind=kOutput, calls=%fused_computation.22 | convolution fusion | flops 339479168 | bytes 10652160 | tf_op jit(solution)/shard_map/chrk,crhs->khs/dot_general | solution.py:74
  133.7 5.9 %copy.132 = f32[2048,1,640]{2,0,1:T(8,128)} copy(f32[2048,1,640]{0,2,1:T(8,128)} %bitcast.84) | data formatting | bytes 10485760 | tf_op jit(solution)/shard_map/stack;reshape | solution.py:77
  139.6 8.8 %pad_maximum_fusion = f32[2048,2,640]{2,0,1:T(8,128)} fusion(f32[2048,1,640]{2,0,1:T(8,128)} %copy.132, f32[2048,1,640]{2,0,1:T(8,128)} %copy.131), kind=kLoop, calls=%fused_computation.2 | loop fusion | flops 2621440 | bytes 20971520 | tf_op jit(solution)/shard_map/stack | solution.py:77
  152.4 9.5 %fusion.29 = (f32[5,256]{1,0:T(8,128)S(1)}, f32[5,256,2048]{2,1,0:T(8,128)}) fusion(f32[256,2048]{1,0:T(8,128)} %compare_select_fusion, bf16[256,5,128]{0,2,1:T(8,128)(2,1)S(1)} %bitcast.87, bf16[2048,5,128]{0,2,1:T(8,128)(2,1)} %bitcast.104), kind=kOutput, calls=%fused_computation.62 | convolution fusion | flops 681576448 | bytes 15537152 | tf_op jit(solution)/shard_map/while/body/eval_jaxpr/sub | solution.py:44
  161.8 27.1 %all-gather.13.cloned.1.call-done = bf16[1,2048,640]{1,2,0:T(8,128)(2,1)} async-done(((bf16[1,128,640]{1,2,0:T(8,128)(2,1)}), bf16[1,2048,640]{1,2,0:T(8,128)(2,1)}) %all-gather.13.cloned.1.call-update) | async-done | bytes 2621456 | tf_op jit(solution)/shard_map/all_gather | solution.py:163
  189.0 6.1 %multiply_reduce_fusion = (f32[5,256]{1,0:T(8,128)S(1)}, f32[5,256,2048]{2,1,0:T(8,128)S(1)}) fusion(f32[5,256,2048]{2,1,0:T(8,128)} %get-tuple-element.90, f32[5,256]{1,0:T(8,128)S(1)} %get-tuple-element.89, bf16[256,5,128]{0,2,1:T(8,128)(2,1)S(1)} %bitcast.96, bf16[2048,5,128]{0,2,1:T(8,128)(2,1)} %bitcast.106), kind=kOutput, calls=%fused_computation.5 | convolution fusion | flops 678951680 | bytes 23930880 | tf_op jit(solution)/shard_map/while/body/eval_jaxpr/rhs,khs->hrk/dot_general | solution.py:48
  202.6 5.9 %copy.143 = f32[2048,1,640]{2,0,1:T(8,128)} copy(f32[2048,1,640]{0,2,1:T(8,128)} %bitcast.78) | data formatting | bytes 10485760 | tf_op jit(solution)/shard_map/stack;reshape | solution.py:77
  208.5 7.4 %fusion.3 = f32[5,2048,128]{1,2,0:T(8,128)} fusion(bf16[256,5,128]{0,2,1:T(8,128)(2,1)S(1)} %bitcast.97, f32[5,256,2048]{2,1,0:T(8,128)} %get-tuple-element.90, f32[5,256]{1,0:T(8,128)S(1)} %get-tuple-element.89), kind=kOutput, calls=%fused_computation.9 | convolution fusion | flops 676331520 | bytes 16061440 | tf_op jit(solution)/shard_map/chrk,crhs->khs/dot_general | solution.py:74
  215.9 5.9 %copy.144 = f32[2048,1,640]{2,0,1:T(8,128)} copy(f32[2048,1,640]{0,2,1:T(8,128)} %bitcast.85) | data formatting | bytes 10485760 | tf_op jit(solution)/shard_map/stack;reshape | solution.py:77
  221.9 8.7 %pad_maximum_fusion.1 = f32[2048,2,640]{2,0,1:T(8,128)} fusion(f32[2048,1,640]{2,0,1:T(8,128)} %copy.144, f32[2048,1,640]{2,0,1:T(8,128)} %copy.143), kind=kLoop, calls=%fused_computation.3 | loop fusion | flops 2621440 | bytes 20971520 | tf_op jit(solution)/shard_map/stack | solution.py:77
  230.6 5.3 %fusion.14 = bf16[5,256,128]{1,2,0:T(8,128)(2,1)S(1)} fusion(bf16[5,256,2048]{2,1,0:T(8,128)(2,1)} %copy-done.2, bf16[2048,5,128]{0,2,1:T(8,128)(2,1)} %bitcast.105), kind=kOutput, calls=%fused_computation.31 | convolution fusion | flops 671416320 | bytes 8192000 | tf_op jit(solution)/shard_map/while/body/eval_jaxpr/hrk,khs->rhs/dot_general | solution.py:55
  236.9 129.5 %psum.7 = f32[2,5]{1,0:T(2,128)S(1)} all-reduce(f32[2,5]{1,0:T(2,128)S(1)} %maximum_negate_fusion), channel_id=1, replica_groups=mesh['seq'=16,'head'=4,'dp'=4] {'seq','dp'}, use_global_device_ids=true, to_apply=%region_10.11 | all-reduce | flops 10 | bytes 80 | tf_op jit(solution)/shard_map/psum | solution.py:160
  369.9 4.8 %all-to-all-start.4 = ((bf16[4,32,640]{2,1,0:T(8,128)(2,1)}), bf16[4,32,640]{2,1,0:T(8,128)(2,1)S(1)}, u32[]{:S(2)}, u32[]{:S(2)}) async-start(bf16[4,32,640]{2,1,0:T(8,128)(2,1)} %convert_element_type.95), calls=%async_computation.4 | async-start | bytes 327680 | tf_op jit(solution)/shard_map/all_to_all | solution.py:146
  379.4 4.8 %all-to-all-start.5 = ((bf16[4,32,640]{2,1,0:T(8,128)(2,1)}), bf16[4,32,640]{2,1,0:T(8,128)(2,1)S(1)}, u32[]{:S(2)}, u32[]{:S(2)}) async-start(bf16[4,32,640]{2,1,0:T(8,128)(2,1)} %bitcast.21), calls=%async_computation.6 | async-start | bytes 327680 | tf_op jit(solution)/shard_map/all_to_all | solution.py:153
  388.9 4.8 %all-to-all-start.6 = ((bf16[4,32,640]{2,1,0:T(8,128)(2,1)}), bf16[4,32,640]{2,1,0:T(8,128)(2,1)S(1)}, u32[]{:S(2)}, u32[]{:S(2)}) async-start(bf16[4,32,640]{2,1,0:T(8,128)(2,1)} %bitcast.23), calls=%async_computation.7 | async-start | bytes 327680 | tf_op jit(solution)/shard_map/all_to_all | solution.py:156
  (101 shorter events, 61.8 us)
Async XLA Ops:
  7.2 143.6 %copy-start = (s32[1,4096]{1,0:T(1,128)S(1)}, s32[1,4096]{1,0:T(1,128)}, u32[]{:S(2)}) copy-start(s32[1,4096]{1,0:T(1,128)} %param.23) | copy-start | bytes 49156
  7.2 36.3 %copy-start.9 = (bf16[1,32,2560]{2,1,0:T(8,128)(2,1)S(1)}, bf16[1,32,2560]{2,1,0:T(8,128)(2,1)}, u32[]{:S(2)}) copy-start(bf16[1,32,2560]{2,1,0:T(8,128)(2,1)} %param.15) | copy-start | bytes 491524
  7.2 41.8 %copy-start.10 = (f32[2,5]{1,0:T(2,128)S(1)}, f32[2,5]{1,0:T(2,128)}, u32[]{:S(2)}) copy-start(f32[2,5]{1,0:T(2,128)} %param.20) | copy-start | bytes 124
  7.2 53.1 %all-gather.7.cloned.1.call-start = ((), (), s32[]{:S(2)}) async-start(), calls=%async_computation.9 | async-start | bytes 2785280 | tf_op jit(solution)/shard_map/all_gather | solution.py:104
  18.3 82.7 %all-gather.9.cloned.1.call-start = ((), (), s32[]{:S(2)}) async-start(), calls=%async_computation.10 | async-start | bytes 2785280 | tf_op jit(solution)/shard_map/all_gather | solution.py:105
  28.6 123.8 %all-gather.11.cloned.1.call-start = ((), (), s32[]{:S(2)}) async-start(), calls=%async_computation.13 | async-start | bytes 2785280 | tf_op jit(solution)/shard_map/all_gather | solution.py:162
  32.1 12.1 %all-to-all-start = ((bf16[32,4,640]{2,0,1:T(8,128)(2,1)}), bf16[32,4,640]{2,0,1:T(8,128)(2,1)S(1)}, u32[]{:S(2)}, u32[]{:S(2)}) async-start(bf16[32,4,640]{2,0,1:T(8,128)(2,1)} %copy.116), calls=%async_computation | async-start | bytes 327680 | tf_op jit(solution)/shard_map/all_to_all | solution.py:96
  36.8 152.2 %all-gather.13.cloned.1.call-start = ((), (), s32[]{:S(2)}) async-start(), calls=%async_computation.14 | async-start | bytes 2785280 | tf_op jit(solution)/shard_map/all_gather | solution.py:163
  44.2 9.5 %all-to-all-start.2 = ((bf16[32,4,640]{2,0,1:T(8,128)(2,1)}), bf16[32,4,640]{2,0,1:T(8,128)(2,1)S(1)}, u32[]{:S(2)}, u32[]{:S(2)}) async-start(bf16[32,4,640]{2,0,1:T(8,128)(2,1)} %copy.121), calls=%async_computation.2 | async-start | bytes 327680 | tf_op jit(solution)/shard_map/all_to_all | solution.py:99
  49.0 325.7 %reduce-scatter.3.cloned.1.call-start = ((), (), s32[]{:S(2)}) async-start(), calls=%async_computation.11 | async-start | bytes 11141120 | tf_op jit(solution)/shard_map/reduce_scatter | solution.py:131
  63.3 45.8 %copy-start.3 = (bf16[2048,640]{0,1:T(8,128)(2,1)}, bf16[2048,640]{0,1:T(8,128)(2,1)S(1)}, u32[]{:S(2)}) copy-start(bf16[2048,640]{0,1:T(8,128)(2,1)S(1)} %copy.118) | copy-start | bytes 7864324
  109.1 2.7 copy-start.4
  109.1 3.6 copy-start.7
  112.7 1.3 copy-start.5
  112.7 1.6 copy-start.6
  148.5 237.1 %reduce-scatter.5.cloned.1.call-start = ((), (), s32[]{:S(2)}) async-start(), calls=%async_computation.12 | async-start | bytes 11141120 | tf_op jit(solution)/shard_map/reduce_scatter | solution.py:193
  189.0 6.1 %slice-start = ((s8[10485760]{0:T(1024)(128)(4,1)}), s8[4194304]{0:T(1024)(128)(4,1)S(1)}, s32[]{:S(2)}) async-start(s8[10485760]{0:T(1024)(128)(4,1)} %bitcast.80), calls=%async_computation.15 | async-start | bytes 8388608
  189.0 7.3 %slice-start.1 = ((s8[10485760]{0:T(1024)(128)(4,1)}), s8[4194304]{0:T(1024)(128)(4,1)S(1)}, s32[]{:S(2)}) async-start(s8[10485760]{0:T(1024)(128)(4,1)} %bitcast.80), calls=%async_computation.16 | async-start | bytes 8388608
  189.0 7.9 %slice-start.2 = ((s8[10485760]{0:T(1024)(128)(4,1)}), s8[2097152]{0:T(1024)(128)(4,1)S(1)}, s32[]{:S(2)}) async-start(s8[10485760]{0:T(1024)(128)(4,1)} %bitcast.80), calls=%async_computation.17 | async-start | bytes 4194304
  198.6 4.0 copy-start.2
  236.9 162.3 %copy-start.1 = (s32[1,4096]{1,0:T(1,128)S(1)}, s32[1,4096]{1,0:T(1,128)}, u32[]{:S(2)}) copy-start(s32[1,4096]{1,0:T(1,128)} %param.23) | copy-start | bytes 49156
  369.9 9.5 %all-to-all-start.4 = ((bf16[4,32,640]{2,1,0:T(8,128)(2,1)}), bf16[4,32,640]{2,1,0:T(8,128)(2,1)S(1)}, u32[]{:S(2)}, u32[]{:S(2)}) async-start(bf16[4,32,640]{2,1,0:T(8,128)(2,1)} %convert_element_type.95), calls=%async_computation.4 | async-start | bytes 327680 | tf_op jit(solution)/shard_map/all_to_all | solution.py:146
  379.4 9.5 %all-to-all-start.5 = ((bf16[4,32,640]{2,1,0:T(8,128)(2,1)}), bf16[4,32,640]{2,1,0:T(8,128)(2,1)S(1)}, u32[]{:S(2)}, u32[]{:S(2)}) async-start(bf16[4,32,640]{2,1,0:T(8,128)(2,1)} %bitcast.21), calls=%async_computation.6 | async-start | bytes 327680 | tf_op jit(solution)/shard_map/all_to_all | solution.py:153
  388.9 9.5 %all-to-all-start.6 = ((bf16[4,32,640]{2,1,0:T(8,128)(2,1)}), bf16[4,32,640]{2,1,0:T(8,128)(2,1)S(1)}, u32[]{:S(2)}, u32[]{:S(2)}) async-start(bf16[4,32,640]{2,1,0:T(8,128)(2,1)} %bitcast.23), calls=%async_computation.7 | async-start | bytes 327680 | tf_op jit(solution)/shard_map/all_to_all | solution.py:156
  (1 other events, 1.0 us)
Sparse Core Ops, SparseCore 0:
  18.5 41.7 all-gather.6
  62.1 38.8 all-gather.8
  103.4 41.4 all-gather.10
  147.0 41.9 all-gather.12
  191.4 73.8 reduce-scatter.2
  267.7 74.0 reduce-scatter.4
where the time goes:
time: 408 us; the launch traced here: 406 us
  blocking collectives  149 us (37%)
  waiting for transfers between devices  83.5 us (20%)
  local copies, waits for them, and re-layouts  52.1 us (13%)
  matrix products  50.7 us (12%)
  other arithmetic  32.3 us (8%)
  starting transfers between devices  24.2 us (6%)
  between operations  14.4 us (4%)
    psum x1, blocking collectives, local(): slope_grad = lax.psum(slope_local, ('seq', 'dp')) / patch_total  129 us
    all_gather x1, waiting for transfers between devices, local(): lax.all_gather(local_values, 'seq', axis=0, tiled=True)  37.8 us
    all_gather x1, waiting for transfers between devices, local(): lax.all_gather(memory_values[0], 'seq', axis=0, tiled=True)  27.1 us
    another operation x4, local copies, waits for them, and re-layouts, key_terms(): jnp.stack([key_grad.reshape(row_count, -1), value_grad.reshape(row_count,...  23.7 us
    another operation x2, other arithmetic, key_terms(): jnp.stack([key_grad.reshape(row_count, -1), value_grad.reshape(row_count,...  17.5 us
    dot_general x2, matrix products, key_terms(): jnp.einsum('chrk,crhs->khs', softmax_b, grad_rows, preferred_element_type...  15.4 us
    unnamed x33, local copies, waits for them, and re-layouts  10.6 us
    all_to_all x1, blocking collectives, local(): lax.all_to_all(self_keys[0], 'head', split_axis=1, concat_axis=0, tiled=T...  10 us
  transfers between devices with their start and end apart: 11, of which 7 were waited for; matrix products, arithmetic and copies ran while one was open for 31% of the time, Pallas kernels for 0%

commit v1 on v0

--- a/solution.py
+++ b/solution.py
@@ -157,7 +157,7 @@
             self_dv.astype(jnp.bfloat16), "head", split_axis=0, concat_axis=1, tiled=True
         ),
     )
-    slope_grad = lax.psum(slope_local, ("seq", "dp")) / patch_total
+    slope_grad = lax.psum(lax.psum(slope_local, "dp"), "seq") / patch_total
     memory_all_keys, memory_all_values = (
         lax.all_gather(memory_keys[0], "seq", axis=0, tiled=True),
         lax.all_gather(memory_values[0], "seq", axis=0, tiled=True),

time: 408 us -> 362 us (0.89)
  blocking collectives: 149 us -> 53.9 us
  waiting for transfers between devices: 83.5 us -> 132 us
    psum x1 -> x2, blocking collectives: 129 us -> 34.6 us  [local(): slope_grad = lax.psum(lax.psum(slope_local, 'dp'), 'seq') / patch_total]
    reduce_scatter x1, waiting for transfers between devices: 0.01 us -> 50.7 us  [local(): lax.psum_scatter(key_terms(text_ds_b, text_p_b, text_query_blocks, text_g...]
  transfers between devices with their start and end apart: 11 -> 11, of which waited for: 7 -> 7; matrix products, arithmetic and copies ran while one was open for 31% -> 35% of each run, Pallas kernels for 0% -> 0%
where the time goes in v1:
time: 362 us; the launch traced here: 360 us
  waiting for transfers between devices  132 us (36%)
  blocking collectives  53.9 us (15%)
  local copies, waits for them, and re-layouts  52.2 us (14%)
  matrix products  50.7 us (14%)
  other arithmetic  32.3 us (9%)
  starting transfers between devices  24.3 us (7%)
  between operations  14.4 us (4%)
    reduce_scatter x1, waiting for transfers between devices, local(): lax.psum_scatter(key_terms(text_ds_b, text_p_b, text_query_blocks, text_g...  50.7 us
    all_gather x1, waiting for transfers between devices, local(): lax.all_gather(local_values, 'seq', axis=0, tiled=True)  37.8 us
    psum x2, blocking collectives, local(): slope_grad = lax.psum(lax.psum(slope_local, 'dp'), 'seq') / patch_total  34.6 us
    all_gather x1, waiting for transfers between devices, local(): lax.all_gather(memory_values[0], 'seq', axis=0, tiled=True)  27.1 us
    another operation x4, local copies, waits for them, and re-layouts, key_terms(): jnp.stack([key_grad.reshape(row_count, -1), value_grad.reshape(row_count,...  23.7 us
    another operation x2, other arithmetic, key_terms(): jnp.stack([key_grad.reshape(row_count, -1), value_grad.reshape(row_count,...  17.5 us
    dot_general x2, matrix products, key_terms(): jnp.einsum('chrk,crhs->khs', softmax_b, grad_rows, preferred_element_type...  15.4 us
    unnamed x33, local copies, waits for them, and re-layouts  10.6 us
  transfers between devices with their start and end apart: 11, of which 7 were waited for; matrix products, arithmetic and copies ran while one was open for 35% of the time, Pallas kernels for 0%

profile of v1, /device:TPU:2, one launch (start us, length us, event | category | flops | bytes accessed | tf_op | source)
XLA Modules:
  0.0 359.8 jit_solution(4920166462424637193)
XLA Ops:
  8.3 10.0 %all_to_all.109 = bf16[32,4,640]{2,0,1:T(8,128)(2,1)} all-to-all(bf16[32,4,640]{2,0,1:T(8,128)(2,1)S(1)} %copy.117), channel_id=1, replica_groups=mesh['seq'=16,'head'=4,'dp'=4] {'head'}, dimensions={1} | all-to-all | bytes 327680 | tf_op jit(solution)/shard_map/all_to_all | solution.py:97
  19.4 9.2 %all_to_all.110 = bf16[32,4,640]{2,0,1:T(8,128)(2,1)} all-to-all(bf16[32,4,640]{2,0,1:T(8,128)(2,1)S(1)} %copy.122), channel_id=1, replica_groups=mesh['seq'=16,'head'=4,'dp'=4] {'head'}, dimensions={1} | all-to-all | bytes 327680 | tf_op jit(solution)/shard_map/all_to_all | solution.py:98
  32.1 4.7 %all-to-all-start = ((bf16[32,4,640]{2,0,1:T(8,128)(2,1)}), bf16[32,4,640]{2,0,1:T(8,128)(2,1)S(1)}, u32[]{:S(2)}, u32[]{:S(2)}) async-start(bf16[32,4,640]{2,0,1:T(8,128)(2,1)} %copy.116), calls=%async_computation | async-start | bytes 327680 | tf_op jit(solution)/shard_map/all_to_all | solution.py:96
  44.2 4.8 %all-to-all-start.2 = ((bf16[32,4,640]{2,0,1:T(8,128)(2,1)}), bf16[32,4,640]{2,0,1:T(8,128)(2,1)S(1)}, u32[]{:S(2)}, u32[]{:S(2)}) async-start(bf16[32,4,640]{2,0,1:T(8,128)(2,1)} %copy.121), calls=%async_computation.2 | async-start | bytes 327680 | tf_op jit(solution)/shard_map/all_to_all | solution.py:99
  54.1 6.2 %all-gather.7.cloned.1.call-done = bf16[2048,640]{1,0:T(8,128)(2,1)} async-done(((bf16[128,640]{1,0:T(8,128)(2,1)}), bf16[2048,640]{1,0:T(8,128)(2,1)}) %all-gather.7.cloned.1.call-update) | async-done | bytes 2621456 | tf_op jit(solution)/shard_map/all_gather | solution.py:104
  63.3 37.8 %all-gather.9.cloned.1.call-done = bf16[2048,640]{1,0:T(8,128)(2,1)} async-done(((bf16[128,640]{1,0:T(8,128)(2,1)}), bf16[2048,640]{1,0:T(8,128)(2,1)}) %all-gather.9.cloned.1.call-update) | async-done | bytes 2621456 | tf_op jit(solution)/shard_map/all_gather | solution.py:105
  119.9 6.0 %copy.131 = f32[2048,1,640]{2,0,1:T(8,128)} copy(f32[2048,1,640]{0,2,1:T(8,128)} %bitcast.79) | data formatting | bytes 10485760 | tf_op jit(solution)/shard_map/stack;reshape | solution.py:77
  125.9 8.0 %fusion.7 = f32[5,2048,128]{1,2,0:T(8,128)} fusion(bf16[128,5,128]{0,2,1:T(8,128)(2,1)S(1)} %copy.130, f32[5,128]{1,0:T(8,128)S(1)} %get-tuple-element.85, f32[5,128,2048]{2,1,0:T(8,128)} %copy-done.4), kind=kOutput, calls=%fused_computation.22 | convolution fusion | flops 339479168 | bytes 10652160 | tf_op jit(solution)/shard_map/chrk,crhs->khs/dot_general | solution.py:74
  133.8 5.9 %copy.132 = f32[2048,1,640]{2,0,1:T(8,128)} copy(f32[2048,1,640]{0,2,1:T(8,128)} %bitcast.84) | data formatting | bytes 10485760 | tf_op jit(solution)/shard_map/stack;reshape | solution.py:77
  139.7 8.8 %pad_maximum_fusion = f32[2048,2,640]{2,0,1:T(8,128)} fusion(f32[2048,1,640]{2,0,1:T(8,128)} %copy.132, f32[2048,1,640]{2,0,1:T(8,128)} %copy.131), kind=kLoop, calls=%fused_computation.2 | loop fusion | flops 2621440 | bytes 20971520 | tf_op jit(solution)/shard_map/stack | solution.py:77
  152.4 9.5 %fusion.29 = (f32[5,256]{1,0:T(8,128)S(1)}, f32[5,256,2048]{2,1,0:T(8,128)}) fusion(f32[256,2048]{1,0:T(8,128)} %compare_select_fusion, bf16[256,5,128]{0,2,1:T(8,128)(2,1)S(1)} %bitcast.87, bf16[2048,5,128]{0,2,1:T(8,128)(2,1)} %bitcast.104), kind=kOutput, calls=%fused_computation.62 | convolution fusion | flops 681576448 | bytes 15537152 | tf_op jit(solution)/shard_map/while/body/eval_jaxpr/sub | solution.py:44
  161.9 27.1 %all-gather.13.cloned.1.call-done = bf16[1,2048,640]{1,2,0:T(8,128)(2,1)} async-done(((bf16[1,128,640]{1,2,0:T(8,128)(2,1)}), bf16[1,2048,640]{1,2,0:T(8,128)(2,1)}) %all-gather.13.cloned.1.call-update) | async-done | bytes 2621456 | tf_op jit(solution)/shard_map/all_gather | solution.py:163
  189.0 6.1 %multiply_reduce_fusion = (f32[5,256]{1,0:T(8,128)S(1)}, f32[5,256,2048]{2,1,0:T(8,128)S(1)}) fusion(f32[5,256,2048]{2,1,0:T(8,128)} %get-tuple-element.90, f32[5,256]{1,0:T(8,128)S(1)} %get-tuple-element.89, bf16[256,5,128]{0,2,1:T(8,128)(2,1)S(1)} %bitcast.96, bf16[2048,5,128]{0,2,1:T(8,128)(2,1)} %bitcast.106), kind=kOutput, calls=%fused_computation.5 | convolution fusion | flops 678951680 | bytes 23930880 | tf_op jit(solution)/shard_map/while/body/eval_jaxpr/rhs,khs->hrk/dot_general | solution.py:48
  202.6 5.9 %copy.143 = f32[2048,1,640]{2,0,1:T(8,128)} copy(f32[2048,1,640]{0,2,1:T(8,128)} %bitcast.78) | data formatting | bytes 10485760 | tf_op jit(solution)/shard_map/stack;reshape | solution.py:77
  208.5 7.4 %fusion.3 = f32[5,2048,128]{1,2,0:T(8,128)} fusion(bf16[256,5,128]{0,2,1:T(8,128)(2,1)S(1)} %bitcast.97, f32[5,256,2048]{2,1,0:T(8,128)} %get-tuple-element.90, f32[5,256]{1,0:T(8,128)S(1)} %get-tuple-element.89), kind=kOutput, calls=%fused_computation.9 | convolution fusion | flops 676331520 | bytes 16061440 | tf_op jit(solution)/shard_map/chrk,crhs->khs/dot_general | solution.py:74
  215.9 5.9 %copy.144 = f32[2048,1,640]{2,0,1:T(8,128)} copy(f32[2048,1,640]{0,2,1:T(8,128)} %bitcast.85) | data formatting | bytes 10485760 | tf_op jit(solution)/shard_map/stack;reshape | solution.py:77
  221.9 8.7 %pad_maximum_fusion.1 = f32[2048,2,640]{2,0,1:T(8,128)} fusion(f32[2048,1,640]{2,0,1:T(8,128)} %copy.144, f32[2048,1,640]{2,0,1:T(8,128)} %copy.143), kind=kLoop, calls=%fused_computation.3 | loop fusion | flops 2621440 | bytes 20971520 | tf_op jit(solution)/shard_map/stack | solution.py:77
  230.6 5.3 %fusion.14 = bf16[5,256,128]{1,2,0:T(8,128)(2,1)S(1)} fusion(bf16[5,256,2048]{2,1,0:T(8,128)(2,1)} %copy-done.2, bf16[2048,5,128]{0,2,1:T(8,128)(2,1)} %bitcast.105), kind=kOutput, calls=%fused_computation.31 | convolution fusion | flops 671416320 | bytes 8192000 | tf_op jit(solution)/shard_map/while/body/eval_jaxpr/hrk,khs->rhs/dot_general | solution.py:55
  235.9 10.5 %psum.14 = f32[2,5]{1,0:T(2,128)S(1)} all-reduce(f32[2,5]{1,0:T(2,128)S(1)} %maximum_negate_fusion), channel_id=1, replica_groups=mesh['seq'=16,'head'=4,'dp'=4] {'dp'}, use_global_device_ids=true, to_apply=%region_10.11 | all-reduce | flops 10 | bytes 80 | tf_op jit(solution)/shard_map/psum | solution.py:160
  247.3 24.2 %psum.15 = f32[2,5]{1,0:T(2,128)S(1)} all-reduce(f32[2,5]{1,0:T(2,128)S(1)} %psum.14), channel_id=1, replica_groups=mesh['seq'=16,'head'=4,'dp'=4] {'seq'}, use_global_device_ids=true, to_apply=%region_11.12 | all-reduce | flops 10 | bytes 80 | tf_op jit(solution)/shard_map/psum | solution.py:160
  275.1 4.8 %all-to-all-start.4 = ((bf16[4,32,640]{2,1,0:T(8,128)(2,1)}), bf16[4,32,640]{2,1,0:T(8,128)(2,1)S(1)}, u32[]{:S(2)}, u32[]{:S(2)}) async-start(bf16[4,32,640]{2,1,0:T(8,128)(2,1)} %convert_element_type.95), calls=%async_computation.4 | async-start | bytes 327680 | tf_op jit(solution)/shard_map/all_to_all | solution.py:146
  284.6 4.8 %all-to-all-start.5 = ((bf16[4,32,640]{2,1,0:T(8,128)(2,1)}), bf16[4,32,640]{2,1,0:T(8,128)(2,1)S(1)}, u32[]{:S(2)}, u32[]{:S(2)}) async-start(bf16[4,32,640]{2,1,0:T(8,128)(2,1)} %bitcast.21), calls=%async_computation.6 | async-start | bytes 327680 | tf_op jit(solution)/shard_map/all_to_all | solution.py:153
  290.8 50.7 %reduce-scatter.5.cloned.1.call-done = f32[128,2,640]{2,0,1:T(8,128)} async-done(((f32[2048,2,640]{2,0,1:T(8,128)}), f32[128,2,640]{2,0,1:T(8,128)}) %reduce-scatter.5.cloned.1.call-update) | async-done | bytes 655376 | tf_op jit(solution)/shard_map/reduce_scatter | solution.py:193
  342.6 4.8 %all-to-all-start.6 = ((bf16[4,32,640]{2,1,0:T(8,128)(2,1)}), bf16[4,32,640]{2,1,0:T(8,128)(2,1)S(1)}, u32[]{:S(2)}, u32[]{:S(2)}) async-start(bf16[4,32,640]{2,1,0:T(8,128)(2,1)} %bitcast.23), calls=%async_computation.7 | async-start | bytes 327680 | tf_op jit(solution)/shard_map/all_to_all | solution.py:156
  (102 shorter events, 68.4 us)
Async XLA Ops:
  7.2 143.6 %copy-start = (s32[1,4096]{1,0:T(1,128)S(1)}, s32[1,4096]{1,0:T(1,128)}, u32[]{:S(2)}) copy-start(s32[1,4096]{1,0:T(1,128)} %param.23) | copy-start | bytes 49156
  7.2 36.2 %copy-start.9 = (bf16[1,32,2560]{2,1,0:T(8,128)(2,1)S(1)}, bf16[1,32,2560]{2,1,0:T(8,128)(2,1)}, u32[]{:S(2)}) copy-start(bf16[1,32,2560]{2,1,0:T(8,128)(2,1)} %param.15) | copy-start | bytes 491524
  7.2 41.8 %copy-start.10 = (f32[2,5]{1,0:T(2,128)S(1)}, f32[2,5]{1,0:T(2,128)}, u32[]{:S(2)}) copy-start(f32[2,5]{1,0:T(2,128)} %param.20) | copy-start | bytes 124
  7.2 53.1 %all-gather.7.cloned.1.call-start = ((), (), s32[]{:S(2)}) async-start(), calls=%async_computation.9 | async-start | bytes 2785280 | tf_op jit(solution)/shard_map/all_gather | solution.py:104
  18.3 82.7 %all-gather.9.cloned.1.call-start = ((), (), s32[]{:S(2)}) async-start(), calls=%async_computation.10 | async-start | bytes 2785280 | tf_op jit(solution)/shard_map/all_gather | solution.py:105
  28.6 123.8 %all-gather.11.cloned.1.call-start = ((), (), s32[]{:S(2)}) async-start(), calls=%async_computation.13 | async-start | bytes 2785280 | tf_op jit(solution)/shard_map/all_gather | solution.py:162
  32.1 12.1 %all-to-all-start = ((bf16[32,4,640]{2,0,1:T(8,128)(2,1)}), bf16[32,4,640]{2,0,1:T(8,128)(2,1)S(1)}, u32[]{:S(2)}, u32[]{:S(2)}) async-start(bf16[32,4,640]{2,0,1:T(8,128)(2,1)} %copy.116), calls=%async_computation | async-start | bytes 327680 | tf_op jit(solution)/shard_map/all_to_all | solution.py:96
  36.8 152.1 %all-gather.13.cloned.1.call-start = ((), (), s32[]{:S(2)}) async-start(), calls=%async_computation.14 | async-start | bytes 2785280 | tf_op jit(solution)/shard_map/all_gather | solution.py:163
  44.2 9.5 %all-to-all-start.2 = ((bf16[32,4,640]{2,0,1:T(8,128)(2,1)}), bf16[32,4,640]{2,0,1:T(8,128)(2,1)S(1)}, u32[]{:S(2)}, u32[]{:S(2)}) async-start(bf16[32,4,640]{2,0,1:T(8,128)(2,1)} %copy.121), calls=%async_computation.2 | async-start | bytes 327680 | tf_op jit(solution)/shard_map/all_to_all | solution.py:99
  49.0 230.9 %reduce-scatter.3.cloned.1.call-start = ((), (), s32[]{:S(2)}) async-start(), calls=%async_computation.11 | async-start | bytes 11141120 | tf_op jit(solution)/shard_map/reduce_scatter | solution.py:131
  63.3 45.9 %copy-start.3 = (bf16[2048,640]{0,1:T(8,128)(2,1)}, bf16[2048,640]{0,1:T(8,128)(2,1)S(1)}, u32[]{:S(2)}) copy-start(bf16[2048,640]{0,1:T(8,128)(2,1)S(1)} %copy.118) | copy-start | bytes 7864324
  109.1 2.7 copy-start.4
  109.1 3.6 %copy-start.7 = (bf16[2048,640]{0,1:T(8,128)(2,1)S(1)}, bf16[2048,640]{0,1:T(8,128)(2,1)}, u32[]{:S(2)}) copy-start(bf16[2048,640]{0,1:T(8,128)(2,1)} %copy.123) | copy-start | bytes 7864324
  112.8 1.3 copy-start.5
  112.8 1.6 copy-start.6
  148.5 192.9 %reduce-scatter.5.cloned.1.call-start = ((), (), s32[]{:S(2)}) async-start(), calls=%async_computation.12 | async-start | bytes 11141120 | tf_op jit(solution)/shard_map/reduce_scatter | solution.py:193
  189.0 6.1 %slice-start = ((s8[10485760]{0:T(1024)(128)(4,1)}), s8[4194304]{0:T(1024)(128)(4,1)S(1)}, s32[]{:S(2)}) async-start(s8[10485760]{0:T(1024)(128)(4,1)} %bitcast.80), calls=%async_computation.15 | async-start | bytes 8388608
  189.0 7.3 %slice-start.1 = ((s8[10485760]{0:T(1024)(128)(4,1)}), s8[4194304]{0:T(1024)(128)(4,1)S(1)}, s32[]{:S(2)}) async-start(s8[10485760]{0:T(1024)(128)(4,1)} %bitcast.80), calls=%async_computation.16 | async-start | bytes 8388608
  189.0 7.9 %slice-start.2 = ((s8[10485760]{0:T(1024)(128)(4,1)}), s8[2097152]{0:T(1024)(128)(4,1)S(1)}, s32[]{:S(2)}) async-start(s8[10485760]{0:T(1024)(128)(4,1)} %bitcast.80), calls=%async_computation.17 | async-start | bytes 4194304
  198.6 4.0 %copy-start.2 = (bf16[5,256,2048]{2,1,0:T(8,128)(2,1)}, bf16[5,256,2048]{2,1,0:T(8,128)(2,1)S(1)}, u32[]{:S(2)}) copy-start(bf16[5,256,2048]{2,1,0:T(8,128)(2,1)S(1)} %multiply_convert_fusion) | copy-start | bytes 15728644
  247.3 105.6 %copy-start.1 = (s32[1,4096]{1,0:T(1,128)S(1)}, s32[1,4096]{1,0:T(1,128)}, u32[]{:S(2)}) copy-start(s32[1,4096]{1,0:T(1,128)} %param.23) | copy-start | bytes 49156
  275.1 9.5 %all-to-all-start.4 = ((bf16[4,32,640]{2,1,0:T(8,128)(2,1)}), bf16[4,32,640]{2,1,0:T(8,128)(2,1)S(1)}, u32[]{:S(2)}, u32[]{:S(2)}) async-start(bf16[4,32,640]{2,1,0:T(8,128)(2,1)} %convert_element_type.95), calls=%async_computation.4 | async-start | bytes 327680 | tf_op jit(solution)/shard_map/all_to_all | solution.py:146
  284.6 58.0 %all-to-all-start.5 = ((bf16[4,32,640]{2,1,0:T(8,128)(2,1)}), bf16[4,32,640]{2,1,0:T(8,128)(2,1)S(1)}, u32[]{:S(2)}, u32[]{:S(2)}) async-start(bf16[4,32,640]{2,1,0:T(8,128)(2,1)} %bitcast.21), calls=%async_computation.6 | async-start | bytes 327680 | tf_op jit(solution)/shard_map/all_to_all | solution.py:153
  342.6 9.5 %all-to-all-start.6 = ((bf16[4,32,640]{2,1,0:T(8,128)(2,1)}), bf16[4,32,640]{2,1,0:T(8,128)(2,1)S(1)}, u32[]{:S(2)}, u32[]{:S(2)}) async-start(bf16[4,32,640]{2,1,0:T(8,128)(2,1)} %bitcast.23), calls=%async_computation.7 | async-start | bytes 327680 | tf_op jit(solution)/shard_map/all_to_all | solution.py:156
  (1 other events, 1.0 us)
Sparse Core Ops, SparseCore 0:
  18.4 41.7 all-gather.6
  62.1 38.8 all-gather.8
  103.4 41.4 all-gather.10
  147.0 41.9 all-gather.12
  191.4 73.5 reduce-scatter.2
  267.4 74.0 reduce-scatter.4
